TPU v7x, 32 devices: a whole 2x2x4 slice. The times are simulated.
32 devices in a mesh: pos: 16 (over z, y, x), head: 2 (over core).
Axes of the slice: x: 2, y: 2, z: 4, core: 2. Of those that a mesh axis runs over, the one named last changes fastest.
Arguments:
- token_ids: int32 [16384], P('pos'), may hold values from 0 to 255
- token_table: float32 [256, 1024], replicated, may hold values from -6 to 6
- row_table: float32 [256, 1024], replicated, may hold values from -6 to 6
- col_table: float32 [256, 1024], replicated, may hold values from -6 to 6
- chan_table: float32 [3, 1024], replicated, may hold values from -6 to 6
- w_query: float32 [1024, 1024], P(None, 'head'), as said below
- w_key: float32 [1024, 1024], P(None, 'head'), as said below
- w_value: float32 [1024, 1024], P(None, 'head'), may hold values from -0.1875 to 0.1875
- w_out: float32 [1024, 1024], P('head', 'pos'), may hold values from -0.1875 to 0.1875
- w_in: float32 [1024, 4096], P('pos', 'head'), may hold values from -0.1875 to 0.1875
- w_down: float32 [4096, 1024], P('head', 'pos'), may hold values from -0.09375 to 0.09375
Outputs:
- latent_out: float32 [512, 1024], P('pos')
Inputs may be any that keep to these rules, and one draw needn't show every extreme that they name: `w_query`: entries of order 1024^-0.5 times a few. `w_key`: entries of order 1024^-0.5 times a few, or larger.
All inputs are finite; a program needn't handle non-finite values.
Results may differ from a plain program's by a relative error of at most 0.0003.
Values sent between devices are 32-bit elements; how exact they have to be, the bound alone decides.
A program may use at most 128 MiB of HBM per device.

v0:
```python
import functools

import jax
import jax.numpy as jnp
from jax import lax
from jax.experimental import pallas as pl
from jax.experimental.pallas import tpu as pltpu
from jax.sharding import PartitionSpec as P

HD = 64
IMG = 256
LAT = 512
LOG2E = 1.4426950408889634
ROWS_KEY = 16
ROWS_LAT = 8
EXTRA = 128
NARROW = jnp.bfloat16


def halves(x):
    high = x.astype(NARROW)
    return high, (x - high.astype(jnp.float32)).astype(NARROW)


def mm(a, b, dims=(((1,), (0,)), ((), ()))):
    return lax.dot_general(a, b, dims, preferred_element_type=jnp.float32)


def mm3(a, b, dims=(((1,), (0,)), ((), ()))):
    a_high, a_low = halves(a)
    b_high, b_low = halves(b)
    return mm(a_high, b_high, dims) + (mm(a_high, b_low, dims) + mm(a_low, b_high, dims))


def send(src, dst, sems, at, pos, head):
    copy = pltpu.make_async_remote_copy(
        src_ref=src,
        dst_ref=dst,
        send_sem=sems[0].at[at],
        recv_sem=sems[1].at[at],
        device_id={"pos": pos, "head": head},
        device_id_type=pl.DeviceIdType.MESH,
    )
    copy.start()
    return copy


def greet(partners):
    barrier = pltpu.get_barrier_semaphore()
    for pos, head in partners:
        pl.semaphore_signal(
            barrier,
            inc=1,
            device_id={"pos": pos, "head": head},
            device_id_type=pl.DeviceIdType.MESH,
        )
    pl.semaphore_wait(barrier, len(partners))


def share_kernel(n_pos, own_ref, all_ref, got, send_sem, recv_sem):
    me, head = lax.axis_index("pos"), lax.axis_index("head")
    peers = [(lax.rem(me + k, n_pos), head) for k in range(1, n_pos)]
    greet(peers)
    copies = []
    for k, (peer, _) in enumerate(peers):
        copies.append(send(own_ref, got.at[me], (send_sem, recv_sem), k, peer, head))
    got[me] = own_ref[...]
    for copy in copies:
        copy.wait()
    all_ref[...] = got[...]


def one_hot_t(info, lanes):
    tall = lax.broadcasted_iota(jnp.int32, (IMG, lanes), 0)
    short = lax.broadcasted_iota(jnp.int32, (EXTRA, lanes), 0)
    tok = jnp.where(tall == info[0:1], 1.0, 0.0).astype(NARROW)
    col = jnp.where(tall == info[1:2], 1.0, 0.0).astype(NARROW)
    pair = jnp.where((short == info[2:3]) | (short == info[3:4]), 1.0, 0.0).astype(NARROW)
    return jnp.concatenate([tok, col, pair], axis=0)


def spread_kernel(info_ref, tabs_ref, out_ref):
    lanes = info_ref.shape[1]
    pick = one_hot_t(info_ref[...], lanes)
    total = jnp.zeros((1, lanes), jnp.float32)
    depth = tabs_ref.shape[1]
    step = 256
    for at in range(0, depth, step):
        high, low = halves(tabs_ref[:, at : at + step])
        emb = mm(high, pick, (((0,), (0,)), ((), ()))) + mm(low, pick, (((0,), (0,)), ((), ())))
        total = total + jnp.sum(emb * emb, axis=0, keepdims=True)
    out_ref[...] = lax.rsqrt(total * (1.0 / depth) + 1e-05)


def attend_kernel(
    block, first_masked, n_pos, parts, moves, info_ref, inv_ref, linfo_ref, linv_ref, tabs_ref,
    w_ref, mlp_ref, out_ref, mlp_out_ref, acc_ref, top_ref, kv_ref, q_ref, state_ref, got_ref,
    mlp_send, mlp_recv, own_sem, st_send, st_recv,
):
    me, head = lax.axis_index("pos"), lax.axis_index("head")
    peers = [lax.rem(me + k, n_pos) for k in range(1, n_pos)]
    greet([(peer, head) for peer in peers])
    copies = []
    if moves:
        wide = mlp_ref.shape[1] // n_pos

        def slab(peer):
            return mlp_ref.at[:, pl.ds(pl.multiple_of(peer * wide, wide), wide)]

        for k, peer in enumerate(peers):
            copies.append(
                send(slab(peer), mlp_out_ref.at[me], (mlp_send, mlp_recv), k, peer, head)
            )
        own = pltpu.make_async_copy(slab(me), mlp_out_ref.at[me], own_sem)
        own.start()
        copies.append(own)

    span = info_ref.shape[1]
    w_high, w_low = halves(w_ref[...])
    t_high, t_low = halves(tabs_ref[...])
    table = mm(t_high, w_high) + mm(t_high, w_low) + mm(t_low, w_high)
    table_t = table.T
    kv_high, kv_low = halves(table_t[0 : 2 * HD])
    kv_ref[...] = jnp.concatenate([kv_high, kv_low], axis=0)
    q_high, q_low = halves(table_t[2 * HD : 3 * HD])
    lat_pick = one_hot_t(linfo_ref[...], LAT)
    q_t = mm(q_high, lat_pick) + mm(q_low, lat_pick)
    q = (q_t * linv_ref[...] * (HD**-0.5 * LOG2E)).T
    q_high, q_low = halves(q)
    q_ref[...] = jnp.concatenate([q_high, q_high, q_low, q_low], axis=1)

    top_ref[...] = jnp.full(top_ref.shape, -1e30, jnp.float32)
    acc_ref[...] = jnp.zeros(acc_ref.shape, jnp.float32)

    def step(i, masked):
        at = pl.multiple_of(i * block, block)
        picked = mm(kv_ref[...], one_hot_t(info_ref[:, pl.ds(at, block)], block))
        both = (picked[0 : 2 * HD] + picked[2 * HD : 4 * HD]) * inv_ref[:, pl.ds(at, block)]
        high, low = halves(both)
        keys = jnp.concatenate([high[:HD], low[:HD], high[:HD], low[:HD]], axis=0)
        vals = jnp.concatenate(
            [high[HD:], low[HD:], jnp.ones((2 * HD, block), NARROW)], axis=0
        )
        scores = mm(q_ref[...], keys)
        if masked:
            back = span - at
            lane = lax.broadcasted_iota(jnp.int32, (LAT, block), 1) - back + LAT
            lat = lax.broadcasted_iota(jnp.int32, (LAT, block), 0)
            scores = jnp.where(lane <= lat, scores, -1e30)
        old = top_ref[:, 0:1]
        new = jnp.maximum(old, jnp.max(scores, axis=1, keepdims=True))
        probs = jnp.exp2(scores - new)
        p_high, p_low = halves(probs)
        dims = (((1,), (1,)), ((), ()))
        acc_ref[...] = acc_ref[...] * jnp.exp2(old - new) + (
            mm(p_high, vals, dims) + mm(p_low, vals, dims)
        )
        top_ref[...] = jnp.broadcast_to(new, top_ref.shape)

    last = lax.rem(me, parts) == parts - 1

    def body(i, carry):
        hide = last & (i >= first_masked)

        @pl.when(hide)
        def _():
            step(i, True)

        @pl.when(jnp.logical_not(hide))
        def _():
            step(i, False)

        return carry

    lax.fori_loop(0, span // block, body, 0)
    acc = acc_ref[...]
    state_ref[...] = jnp.concatenate(
        [acc[:, :HD] + acc[:, HD : 2 * HD], acc[:, 2 * HD : 2 * HD + 32], top_ref[:, 0:32]],
        axis=1,
    )
    rows = LAT // n_pos

    def latents_of(peer):
        return pl.ds(pl.multiple_of(peer * rows, rows), rows)

    for k, peer in enumerate(peers):
        copies.append(
            send(state_ref.at[latents_of(peer)], got_ref.at[me], (st_send, st_recv), k, peer, head)
        )
    got_ref[me] = state_ref[latents_of(me), :]
    for copy in copies:
        copy.wait()
    out_ref[...] = got_ref[...]


def mlp_kernel(
    n_pos, heads, outer, part_ref, in_ref, down_ref, out_ref,
    sums, lanes, full, other, other_got, red, red_got, mid, mid_got, last,
    s0, r0, s1, r1, s2, r2, s3, r3, s4, r4, s5, r5, s6, r6, s7, r7,
):
    inner = n_pos // outer
    me, head = lax.axis_index("pos"), lax.axis_index("head")
    z, s = me // inner, lax.rem(me, inner)
    cols = full.shape[-1]
    lat = n_pos * full.shape[3]
    siblings = [lax.rem(head + k, heads) for k in range(1, heads)]
    deep = [lax.rem(z + k, outer) for k in range(1, outer)]
    flat = [lax.rem(s + k, inner) for k in range(1, inner)]
    greet(
        [(me, h) for h in siblings]
        + [(zz * inner + s, head) for zz in deep]
        + [(z * inner + ss, head) for ss in flat]
    )

    sums[head] = part_ref[...]
    copies = [
        send(sums.at[head], sums.at[head], (s0, r0), k, me, h) for k, h in enumerate(siblings)
    ]
    for copy in copies:
        copy.wait()
    projected = sums[0]
    for h in range(1, heads):
        projected = projected + sums[h]
    normed = layer_norm(projected)
    for h in range(heads):
        lanes[h] = normed[:, h * cols : (h + 1) * cols]
    full[head, z, s] = lanes[head]

    mine = full.at[head, z, s]
    copies = [
        send(mine, mine, (s1, r1), k, zz * inner + s, head) for k, zz in enumerate(deep)
    ]
    for copy in copies:
        copy.wait()
    mine = full.at[head, :, s]
    copies = [
        send(mine, mine, (s2, r2), k, z * inner + ss, head) for k, ss in enumerate(flat)
    ]
    across = [
        send(mine, mine, (s3, r3), k * inner, me, h) for k, h in enumerate(siblings)
    ]
    for j, copy in enumerate(copies):
        copy.wait()
        came = full.at[head, :, lax.rem(s - (j + 1) + inner, inner)]
        across += [
            send(came, came, (s3, r3), k * inner + j + 1, me, h)
            for k, h in enumerate(siblings)
        ]

    def weights(h):
        return pl.ds(pl.multiple_of(h * cols, cols), cols)

    def hidden_from(h):
        return mm3(full[h].reshape(lat, cols), in_ref[weights(h), :])

    hidden = hidden_from(head)
    for copy in across:
        copy.wait()
    for h in siblings:
        hidden = hidden + hidden_from(h)
    cube = hidden * hidden * hidden
    hidden = 0.5 * hidden * (1.0 + jnp.tanh(0.7978845608028654 * (hidden + 0.044715 * cube)))

    def down_to(h):
        return mm3(hidden, down_ref[weights(h), :], (((1,), (1,)), ((), ())))

    copies = []
    for k, h in enumerate(siblings):
        other[k] = down_to(h)
        copies.append(send(other.at[k], other_got.at[k], (s4, r4), k, me, h))
    total = down_to(head)
    for k, copy in enumerate(copies):
        copy.wait()
        total = total + other_got[k]
    red[...] = total.reshape(red.shape)

    copies = [
        send(red.at[:, ss], red_got.at[k], (s5, r5), k, z * inner + ss, head)
        for k, ss in enumerate(flat)
    ]
    total = red[:, s]
    for k, copy in enumerate(copies):
        copy.wait()
        total = total + red_got[k]
    mid[...] = total
    copies = [
        send(mid.at[zz], mid_got.at[k], (s6, r6), k, zz * inner + s, head)
        for k, zz in enumerate(deep)
    ]
    total = mid[z]
    for k, copy in enumerate(copies):
        copy.wait()
        total = total + mid_got[k]
    last[head] = total
    copies = [
        send(last.at[head], last.at[head], (s7, r7), k, me, h) for k, h in enumerate(siblings)
    ]
    for copy in copies:
        copy.wait()
    out_ref[...] = projected + jnp.concatenate([last[h] for h in range(heads)], axis=1)


def layer_norm(values):
    center = values - jnp.mean(values, axis=-1, keepdims=True)
    spread = jnp.mean(center * center, axis=-1, keepdims=True)
    return center * lax.rsqrt(spread + 1e-05)


def describe(ids, where, row_at, row_first, chan_at):
    pixel = where // 3
    return jnp.stack(
        [ids, pixel % IMG, pixel // IMG - row_first + row_at, where % 3 + chan_at]
        + [jnp.zeros_like(ids)] * 4
    )


def per_device(
    token_ids,
    token_table,
    row_table,
    col_table,
    chan_table,
    w_query,
    w_key,
    w_value,
    w_out,
    w_in,
    w_down,
):
    high = lax.Precision.HIGH
    local = token_ids.shape[0]
    n_pos = lax.axis_size("pos")
    index = lax.axis_index("pos")
    total = local * n_pos
    heads_dev = w_key.shape[1] // HD
    parts = n_pos // heads_dev
    span = total // parts
    head, part = index // parts, index % parts
    depth = token_table.shape[1]

    def centered(table):
        return table - jnp.mean(table, axis=-1, keepdims=True)

    row_mid = centered(row_table)

    def rows_from(start, count):
        first = jnp.minimum(start // 3 // IMG, row_table.shape[0] - count)
        return first, lax.dynamic_slice_in_dim(row_mid, first, count)

    own_first, own_rows = rows_from(index * local, ROWS_KEY)
    key_first, key_rows = rows_from(part * span, ROWS_KEY)
    lat_first, lat_rows_tab = rows_from(jnp.int32(total - LAT), ROWS_LAT)
    base = [centered(token_table), centered(col_table)]
    tail = [
        lat_rows_tab,
        centered(chan_table),
        jnp.zeros((EXTRA - ROWS_KEY - ROWS_LAT - 3, depth), jnp.float32),
    ]
    own_tabs = jnp.concatenate(base + [own_rows] + tail)
    tabs = jnp.concatenate(base + [key_rows] + tail)
    chan_at = ROWS_KEY + ROWS_LAT

    own_where = index * local + jnp.arange(local, dtype=jnp.int32)
    own_info = describe(token_ids, own_where, 0, own_first, chan_at)
    inv = pl.pallas_call(
        spread_kernel,
        out_shape=jax.ShapeDtypeStruct((1, local), jnp.float32),
        compiler_params=pltpu.CompilerParams(vmem_limit_bytes=48 * 2**20),
    )(own_info, own_tabs)

    vmem = pl.BlockSpec(memory_space=pltpu.VMEM)
    hbm = pl.BlockSpec(memory_space=pl.ANY)
    dma = pltpu.SemaphoreType.DMA
    sent = jnp.concatenate(
        [token_ids.astype(jnp.float32).reshape(-1, 128), inv.reshape(-1, 128)]
    )
    got = pl.pallas_call(
        functools.partial(share_kernel, n_pos),
        out_shape=jax.ShapeDtypeStruct((n_pos,) + sent.shape, jnp.float32),
        in_specs=[vmem],
        out_specs=vmem,
        scratch_shapes=[
            pltpu.VMEM((n_pos,) + sent.shape, jnp.float32),
            dma((n_pos - 1,)),
            dma((n_pos - 1,)),
        ],
        compiler_params=pltpu.CompilerParams(collective_id=0, has_side_effects=True),
    )(sent)
    got = got.reshape(n_pos, 2, local).transpose(1, 0, 2).reshape(2, total)
    all_ids = got[0].astype(jnp.int32)
    key_ids = lax.dynamic_slice_in_dim(all_ids, part * span, span)
    key_inv = lax.dynamic_slice_in_dim(got[1:2], part * span, span, axis=1)
    key_where = part * span + jnp.arange(span, dtype=jnp.int32)
    key_info = describe(key_ids, key_where, 0, key_first, chan_at)
    lat_where = total - LAT + jnp.arange(LAT, dtype=jnp.int32)
    lat_info = describe(all_ids[total - LAT :], lat_where, ROWS_KEY, lat_first, chan_at)
    lat_inv = got[1:2, total - LAT :]

    def of_head(w):
        return lax.dynamic_slice_in_dim(w, head * HD, HD, axis=1)

    w_qkv = jnp.concatenate(
        [of_head(w_key), of_head(w_value), of_head(w_query), jnp.zeros((depth, HD), jnp.float32)],
        axis=1,
    )
    block = min(1024, span)
    first_masked = (span - LAT) // block
    ff_rows = w_in.shape[1] // n_pos
    lat_rows = LAT // n_pos
    moves = ff_rows % 128 == 0
    mlp_weights = jnp.concatenate([w_in, w_down.T])
    if not moves:
        mlp_kept = lax.all_to_all(
            mlp_weights.reshape(-1, n_pos, ff_rows).transpose(1, 0, 2),
            "pos", split_axis=0, concat_axis=0, tiled=True,
        )
        mlp_weights = jnp.zeros((8, 128), jnp.float32)
    mlp_shape = (n_pos, mlp_weights.shape[0], ff_rows) if moves else (8, 128)
    state_shape = (n_pos, lat_rows, 2 * HD)
    states, mlp_moved = pl.pallas_call(
        functools.partial(attend_kernel, block, first_masked, n_pos, parts, moves),
        out_shape=[
            jax.ShapeDtypeStruct(state_shape, jnp.float32),
            jax.ShapeDtypeStruct(mlp_shape, jnp.float32),
        ],
        in_specs=[vmem] * 6 + [hbm],
        out_specs=[vmem, hbm],
        scratch_shapes=[
            pltpu.VMEM((LAT, 4 * HD), jnp.float32),
            pltpu.VMEM((LAT, 128), jnp.float32),
            pltpu.VMEM((4 * HD, 2 * IMG + EXTRA), NARROW),
            pltpu.VMEM((LAT, 4 * HD), NARROW),
            pltpu.VMEM((LAT, 2 * HD), jnp.float32),
            pltpu.VMEM(state_shape, jnp.float32),
            dma((n_pos - 1,)),
            dma((n_pos - 1,)),
            dma,
            dma((n_pos - 1,)),
            dma((n_pos - 1,)),
        ],
        compiler_params=pltpu.CompilerParams(
            vmem_limit_bytes=48 * 2**20, collective_id=1, has_side_effects=True
        ),
        cost_estimate=pl.CostEstimate(
            flops=20 * 10**9, bytes_accessed=8 * 2**20, transcendentals=4 * 2**20
        ),
    )(key_info, key_inv, lat_info, lat_inv, tabs, w_qkv, mlp_weights)
    if moves:
        mlp_kept = mlp_moved
    in_rows = w_in.shape[0]
    my_in = mlp_kept[:, :in_rows].reshape(-1, ff_rows)
    my_down = mlp_kept[:, in_rows:].reshape(-1, ff_rows)

    whole_out = lax.all_gather(w_out, "pos", axis=1, tiled=True)
    states = states.reshape(heads_dev, parts, lat_rows, 2 * HD)
    tops = states[..., 96:97]
    factor = jnp.exp2(tops - jnp.max(tops, axis=1, keepdims=True))
    weight = jnp.sum(states[..., 64:65] * factor, axis=1)
    accum = jnp.sum(states[..., :HD] * factor, axis=1)
    attended = (accum / weight).transpose(1, 0, 2).reshape(lat_rows, heads_dev * HD)
    partial_out = jnp.dot(attended, whole_out, precision=high)

    heads = lax.axis_size("head")
    outer = 4 if n_pos % 4 == 0 else 1
    inner = n_pos // outer
    cols = depth // heads

    def room(*shape):
        return pltpu.VMEM(shape, jnp.float32)

    counts = [heads, outer, inner, heads * inner, heads, inner, outer, heads]
    return pl.pallas_call(
        functools.partial(mlp_kernel, n_pos, heads, outer),
        out_shape=jax.ShapeDtypeStruct((lat_rows, depth), jnp.float32),
        in_specs=[vmem] * 3,
        out_specs=vmem,
        scratch_shapes=[
            room(heads, lat_rows, depth),
            room(heads, lat_rows, cols),
            room(heads, outer, inner, lat_rows, cols),
            room(heads - 1, LAT, cols),
            room(heads - 1, LAT, cols),
            room(outer, inner, lat_rows, cols),
            room(inner - 1, outer, lat_rows, cols),
            room(outer, lat_rows, cols),
            room(outer - 1, lat_rows, cols),
            room(heads, lat_rows, cols),
        ]
        + [dma((count,)) for count in counts for _ in range(2)],
        compiler_params=pltpu.CompilerParams(
            vmem_limit_bytes=48 * 2**20, collective_id=2, has_side_effects=True
        ),
    )(partial_out, my_in, my_down)


def solution(mesh):
    placed = (
        P("pos"),
        P(),
        P(),
        P(),
        P(),
        P(None, "head"),
        P(None, "head"),
        P(None, "head"),
        P("head", "pos"),
        P("pos", "head"),
        P("head", "pos"),
    )
    return jax.shard_map(
        per_device, mesh=mesh, in_specs=placed, out_specs=P("pos", None), check_vma=False
    )
```

profile of v0, /device:TPU:0, one launch (start us, length us, event | category | flops | bytes accessed | tf_op | source)
XLA Modules:
  0.0 166.7 jit_solution(2040448209981136020)
XLA Ops:
  7.5 1.0 and_select_fusion.2
  8.5 1.0 fusion.4
  10.7 1.4 reduce_sum.57
  12.0 1.4 reduce_sum.56
  13.7 1.0 copy-done.5
  14.9 2.7 %broadcast_subtract_fusion.1 = (f32[256,1024]{1,0:T(8,128)S(1)}, f32[256,1024]{1,0:T(8,128)}) fusion(f32[256,1024]{1,0:T(8,128)} %param.14, f32[256]{0:T(256)S(1)} %broadcast_multiply_fusion.1, f32[256,1024]{1,0:T(8,128)} %param.12, f32[256]{0:T(256)S(1)} %broadcast_multiply_fusion.2), kind=kLoop, calls=%fused_computation.3 | loop fusion | flops 524288 | bytes 4196352 | tf_op jit(solution)/shard_map/sub | solution.py:342
  17.6 1.0 constant_dynamic-slice_fusion.3
  18.7 0.8 broadcast_in_dim.4
  19.5 8.6 %concatenate.15.tabs_ref = f32[640,1024]{1,0:T(8,128)} concatenate(f32[256,1024]{1,0:T(8,128)} %get-tuple-element.29, f32[256,1024]{1,0:T(8,128)S(1)} %get-tuple-element.28, f32[16,1024]{1,0:T(8,128)S(1)} %get-tuple-element.12, f32[8,1024]{1,0:T(8,128)S(1)} %dynamic_slice.32, f32[3,1024]{1,0:T(4,128)S(1)} %broadcast_subtract_fusion.3, f32[101,1024]{1,0:T(8,128)} %broadcast_in_dim.4), dimensions={0} | concatenate | bytes 5242880 | tf_op jit(solution)/shard_map/concatenate | solution.py:359
  28.1 1.7 %copy-done.1 = f32[640,1024]{1,0:T(8,128)S(1)} copy-done((f32[640,1024]{1,0:T(8,128)S(1)}, f32[640,1024]{1,0:T(8,128)}, u32[]{:S(2)}) %copy-start.1) | copy-done | bytes 2621464
  29.8 3.7 %shard_map.109 = f32[1,1024]{1,0:T(1,128)S(1)} custom-call(s32[8,1024]{1,0:T(8,128)S(1)} %stack.38.info_ref, f32[640,1024]{1,0:T(8,128)S(1)} %copy-done.1), custom_call_target="tpu_custom_call" | custom-call | tf_op jit(solution)/shard_map/pallas_call | solution.py:365
  34.1 12.2 %shard_map.110 = f32[16,16,128]{2,1,0:T(8,128)} custom-call(f32[16,128]{1,0:T(8,128)} %pad_maximum_fusion.1.own_ref), custom_call_target="tpu_custom_call" | custom-call | tf_op jit(solution)/shard_map/pallas_call | solution.py:377
  46.3 1.0 reshape.399
  48.0 1.3 slice.44
  49.3 1.4 dynamic_slice.26
  50.8 8.6 %concatenate.17.tabs_ref = f32[640,1024]{1,0:T(8,128)} concatenate(f32[256,1024]{1,0:T(8,128)} %get-tuple-element.29, f32[256,1024]{1,0:T(8,128)S(1)} %get-tuple-element.28, f32[16,1024]{1,0:T(8,128)S(1)} %get-tuple-element.11, f32[8,1024]{1,0:T(8,128)S(1)} %dynamic_slice.32, f32[3,1024]{1,0:T(4,128)S(1)} %broadcast_subtract_fusion.3, f32[101,1024]{1,0:T(8,128)} %broadcast_in_dim.4), dimensions={0} | concatenate | bytes 5242880 | tf_op jit(solution)/shard_map/concatenate | solution.py:360
  59.7 1.6 constant_dynamic-slice_fusion
  61.8 1.0 stack.41.info_ref
  62.8 1.3 pad_maximum_fusion.mlp_ref
  64.2 37.9 %shard_map.111 = (f32[16,32,128]{2,1,0:T(8,128)S(1)}, f32[16,128,128]{2,1,0:T(8,128)S(1)}) custom-call(s32[8,8192]{1,0:T(8,128)S(1)} %copy-done.3, f32[1,8192]{1,0:T(1,128)S(1)} %constant_dynamic-slice_fusion.4.inv_ref, s32[8,512]{1,0:T(8,128)S(1)} %stack.44.linfo_ref, f32[1,512]{1,0:T(1,128)S(1)} %slice.45.linv_ref, f32[640,1024]{1,0:T(8,128)} %concatenate.17.tabs_ref, ...), custom_call_target="tpu_custom_call" | custom-call | flops 20000000000 | bytes 8388608 | tf_op jit(solution)/shard_map/pallas_call | solution.py:420
  102.1 1.0 copy-done.2
  104.1 1.3 fusion.12
  105.4 2.6 %fusion.14.part_ref = f32[32,1024]{1,0:T(8,128)S(1)} fusion(f32[32,512]{1,0:T(8,128)S(1)} %reshape.402, f32[512,1024]{0,1:T(8,128)} %all-gather.2.cloned.1.call-done), kind=kOutput, calls=%fused_computation.65 | convolution fusion | flops 100663296 | bytes 2293760 | tf_op jit(solution)/shard_map/dot_general | solution.py:461
  108.0 51.2 %shard_map.112 = f32[32,1024]{1,0:T(8,128)S(1)} custom-call(f32[32,1024]{1,0:T(8,128)S(1)} %fusion.14.part_ref, f32[1024,128]{1,0:T(8,128)S(1)} %bitcast.32, f32[1024,128]{1,0:T(8,128)S(1)} %bitcast.31), custom_call_target="tpu_custom_call" | custom-call | tf_op jit(solution)/shard_map/pallas_call | solution.py:472
  (71 shorter events, 6.5 us)
Async XLA Ops:
  6.5 52.9 %copy-start = (f32[1024,512]{1,0:T(8,128)S(1)}, f32[1024,512]{1,0:T(8,128)}, u32[]{:S(2)}) copy-start(f32[1024,512]{1,0:T(8,128)} %param.17) | copy-start | bytes 6291460
  6.5 6.9 %copy-start.4 = (f32[256,1024]{1,0:T(8,128)S(1)}, f32[256,1024]{1,0:T(8,128)}, u32[]{:S(2)}) copy-start(f32[256,1024]{1,0:T(8,128)} %param.13) | copy-start | bytes 3145732
  6.5 98.9 %all-gather.2.cloned.1.call-start = ((), (), s32[]{:S(2)}) async-start(), calls=%async_computation | async-start | bytes 2228224 | tf_op jit(solution)/shard_map/all_gather | solution.py:454
  12.0 2.7 %copy-start.9 = (f32[3,1024]{1,0:T(4,128)S(1)}, f32[3,1024]{1,0:T(4,128)}, u32[]{:S(2)}) copy-start(f32[3,1024]{1,0:T(4,128)} %param.15) | copy-start | bytes 36868
  12.0 2.9 %copy-start.10 = (s32[1024]{0:T(1024)S(1)}, s32[1024]{0:T(1024)}, u32[]{:S(2)}) copy-start(s32[1024]{0:T(1024)} %param.11) | copy-start | bytes 12292
  13.7 1.0 copy-start.5
  28.1 1.7 %copy-start.1 = (f32[640,1024]{1,0:T(8,128)S(1)}, f32[640,1024]{1,0:T(8,128)}, u32[]{:S(2)}) copy-start(f32[640,1024]{1,0:T(8,128)} %concatenate.15.tabs_ref) | copy-start | bytes 7864324
  59.7 2.1 %copy-start.6 = (s32[1,8192]{1,0:T(1,128)S(1)}, s32[1,8192]{1,0:T(1,128)}, u32[]{:S(2)}) copy-start(s32[1,8192]{1,0:T(1,128)} %get-tuple-element.27) | copy-start | bytes 98308
  59.7 2.1 %copy-start.7 = (s32[1,8192]{1,0:T(1,128)S(1)}, s32[1,8192]{1,0:T(1,128)}, u32[]{:S(2)}) copy-start(s32[1,8192]{1,0:T(1,128)} %fusion.4) | copy-start | bytes 98308
  59.7 2.1 %copy-start.8 = (s32[8192]{0:T(1024)S(1)}, s32[8192]{0:T(1024)}, u32[]{:S(2)}) copy-start(s32[8192]{0:T(1024)} %dynamic_slice.26) | copy-start | bytes 98308
  61.3 1.5 copy-start.11
  61.3 1.5 copy-start.12
  61.3 1.5 copy-start.13
  61.3 1.5 copy-start.14
  62.8 1.4 copy-start.3
  102.1 1.0 copy-start.2
Sparse Core Ops, SparseCore 0:
  10.1 77.5 all-gather.1
where the time goes:
time: 167 us
  Pallas kernels  105 us (63%)
  local copies, waits for them, and re-layouts  32.6 us (20%)
  between operations  13.9 us (8%)
  other arithmetic  12 us (7%)
  matrix products  2.6 us (2%)
    pallas_call x1, Pallas kernels, per_device(): pl.pallas_call(functools.partial(mlp_kernel, n_pos, heads, outer), out_sh...  51.2 us
    pallas_call x1, Pallas kernels, per_device(): pl.pallas_call(functools.partial(attend_kernel, block, first_masked, n_po...  37.9 us
    pallas_call x1, Pallas kernels, per_device(): pl.pallas_call(functools.partial(share_kernel, n_pos), out_shape=jax.Shap...  12.2 us
    concatenate x1, local copies, waits for them, and re-layouts, per_device(): own_tabs = jnp.concatenate(base + [own_rows] + tail)  8.62 us
    concatenate x1, local copies, waits for them, and re-layouts, per_device(): tabs = jnp.concatenate(base + [key_rows] + tail)  8.62 us
    unnamed x36, local copies, waits for them, and re-layouts  5.51 us
    pallas_call x1, Pallas kernels, per_device(): pl.pallas_call(spread_kernel, out_shape=jax.ShapeDtypeStruct((1, local),...  3.69 us
  transfers between devices with their start and end apart: 1, of which 0 were waited for; matrix products, arithmetic and copies ran while one was open for 24% of the time, Pallas kernels for 32%

commit v1 on v0

v1 whole, which is shorter than its diff:
```python
import functools

import jax
import jax.numpy as jnp
from jax import lax
from jax.experimental import pallas as pl
from jax.experimental.pallas import tpu as pltpu
from jax.sharding import PartitionSpec as P

HD = 64
IMG = 256
LAT = 512
LOG2E = 1.4426950408889634
ROWS_KEY = 24
ROWS_OWN = 16
ROWS_LAT = 16
CHAN_AT = ROWS_KEY + ROWS_OWN + ROWS_LAT
EXTRA = 128
NARROW = jnp.bfloat16


def halves(x):
    high = x.astype(NARROW)
    return high, (x - high.astype(jnp.float32)).astype(NARROW)


def mm(a, b, dims=(((1,), (0,)), ((), ()))):
    return lax.dot_general(a, b, dims, preferred_element_type=jnp.float32)


def mm3(a, b, dims=(((1,), (0,)), ((), ()))):
    a_high, a_low = halves(a)
    b_high, b_low = halves(b)
    return mm(a_high, b_high, dims) + (mm(a_high, b_low, dims) + mm(a_low, b_high, dims))


def send(src, dst, sems, at, pos, head):
    copy = pltpu.make_async_remote_copy(
        src_ref=src,
        dst_ref=dst,
        send_sem=sems[0].at[at],
        recv_sem=sems[1].at[at],
        device_id={"pos": pos, "head": head},
        device_id_type=pl.DeviceIdType.MESH,
    )
    copy.start()
    return copy


def greet(partners):
    barrier = pltpu.get_barrier_semaphore()
    for pos, head in partners:
        pl.semaphore_signal(
            barrier,
            inc=1,
            device_id={"pos": pos, "head": head},
            device_id_type=pl.DeviceIdType.MESH,
        )
    pl.semaphore_wait(barrier, len(partners))


def one_hot_t(ids, where, row_first, row_at):
    lanes = ids.shape[1]
    pixel = jnp.floor((where.astype(jnp.float32) + 0.5) * (1.0 / 3.0)).astype(jnp.int32)
    chan = where - 3 * pixel + CHAN_AT
    row = (pixel >> 8) - row_first + row_at
    column = pixel & (IMG - 1)
    tall = lax.broadcasted_iota(jnp.int32, (IMG, lanes), 0)
    short = lax.broadcasted_iota(jnp.int32, (EXTRA, lanes), 0)
    tok = jnp.where(tall == ids, 1.0, 0.0).astype(NARROW)
    col = jnp.where(tall == column, 1.0, 0.0).astype(NARROW)
    pair = jnp.where((short == row) | (short == chan), 1.0, 0.0).astype(NARROW)
    return jnp.concatenate([tok, col, pair], axis=0)


def front_kernel(
    n_pos, parts, outer, moves,
    ids_ref, tok_ref, row_ref, col_ref, chan_ref, wk_ref, wv_ref, wq_ref, wo_ref, mlp_ref,
    out_ref, wo_out_ref, mlp_out_ref,
    tabs_ref, high_ref, low_ref, w_ref, ids_got, acc_ref, top_ref, kv_ref, q_ref, state_ref,
    got_ref, w_sem, own_sem, id_send, id_recv, wz_send, wz_recv, wp_send, wp_recv,
    mlp_send, mlp_recv, st_send, st_recv,
):
    inner = n_pos // outer
    me, head = lax.axis_index("pos"), lax.axis_index("head")
    z, s = me // inner, lax.rem(me, inner)
    peers = [lax.rem(me + k, n_pos) for k in range(1, n_pos)]
    deep = [lax.rem(z + k, outer) for k in range(1, outer)]
    flat = [lax.rem(s + k, inner) for k in range(1, inner)]
    greet([(peer, head) for peer in peers])
    local = ids_ref.shape[1]
    total = local * n_pos
    span = total // parts
    slot, part = me // parts, lax.rem(me, parts)

    at = pl.multiple_of(slot // 2 * 2 * HD, 2 * HD)
    loads = []
    for k, ref in enumerate((wk_ref, wv_ref, wq_ref)):
        loads.append(
            pltpu.make_async_copy(ref.at[:, pl.ds(at, 2 * HD)], w_ref.at[k], w_sem.at[k])
        )
        loads[-1].start()

    def rows_from(start, count):
        first = start // (3 * IMG) // 8 * 8
        first = jnp.minimum(first, row_ref.shape[0] - count)
        return first, row_ref[pl.ds(pl.multiple_of(first, 8), count), :]

    key_first, key_rows = rows_from(part * span, ROWS_KEY)
    own_first, own_rows = rows_from(me * local, ROWS_OWN)
    lat_first, lat_rows = rows_from(jnp.int32(total - LAT), ROWS_LAT)
    tabs_ref[2 * IMG :, :] = jnp.zeros((EXTRA, tabs_ref.shape[1]), jnp.float32)
    tabs_ref[2 * IMG + CHAN_AT : 2 * IMG + CHAN_AT + 3, :] = chan_ref[...]
    extra = jnp.concatenate([key_rows, own_rows, lat_rows, tabs_ref[2 * IMG + CHAN_AT :, :]])
    for k, table in enumerate((tok_ref[...], col_ref[...], extra)):
        mid = table - jnp.mean(table, axis=1, keepdims=True)
        high, low = halves(mid)
        high_ref[k * IMG : k * IMG + table.shape[0], :] = high
        low_ref[k * IMG : k * IMG + table.shape[0], :] = low

    iota = lax.broadcasted_iota(jnp.int32, (1, local), 1)
    ids = ids_ref[...]
    pick = one_hot_t(ids, me * local + iota, own_first, ROWS_KEY)
    depth = tabs_ref.shape[1]
    square = jnp.zeros((1, local), jnp.float32)
    dims = (((0,), (0,)), ((), ()))
    for c in range(0, depth, 256):
        emb = mm(high_ref[:, c : c + 256], pick, dims) + mm(low_ref[:, c : c + 256], pick, dims)
        square = square + jnp.sum(emb * emb, axis=0, keepdims=True)
    inv = lax.rsqrt(square * (1.0 / depth) + 1e-05)
    ids_got[me] = jnp.concatenate([ids.astype(jnp.float32), inv], axis=0)
    id_copies = [
        send(ids_got.at[me], ids_got.at[me], (id_send, id_recv), k, peer, head)
        for k, peer in enumerate(peers)
    ]

    own = pltpu.make_async_copy(wo_ref, wo_out_ref.at[z, s], own_sem.at[0])
    own.start()
    wz_copies = [
        send(wo_ref, wo_out_ref.at[z, s], (wz_send, wz_recv), k, zz * inner + s, head)
        for k, zz in enumerate(deep)
    ]
    copies = []
    if moves:
        wide = mlp_ref.shape[1] // n_pos

        def slab(peer):
            return mlp_ref.at[:, pl.ds(pl.multiple_of(peer * wide, wide), wide)]

        for k, peer in enumerate(peers):
            copies.append(
                send(slab(peer), mlp_out_ref.at[me], (mlp_send, mlp_recv), k, peer, head)
            )
        kept = pltpu.make_async_copy(slab(me), mlp_out_ref.at[me], own_sem.at[1])
        kept.start()
        copies.append(kept)

    for load in loads:
        load.wait()
    even = lax.rem(slot, 2) == 0
    w = jnp.concatenate(
        [jnp.where(even, w_ref[k][:, :HD], w_ref[k][:, HD:]) for k in range(3)]
        + [jnp.zeros((depth, HD), jnp.float32)],
        axis=1,
    )
    w_high, w_low = halves(w)
    table = (
        mm(high_ref[...], w_high) + mm(high_ref[...], w_low) + mm(low_ref[...], w_high)
    )
    table_t = table.T
    kv_high, kv_low = halves(table_t[0 : 2 * HD])
    kv_ref[...] = jnp.concatenate([kv_high, kv_low], axis=0)
    q_high, q_low = halves(table_t[2 * HD : 3 * HD])
    top_ref[...] = jnp.full(top_ref.shape, -1e30, jnp.float32)
    acc_ref[...] = jnp.zeros(acc_ref.shape, jnp.float32)
    for copy in id_copies:
        copy.wait()

    late = ids_got[n_pos - 1][:, local - LAT :]
    lat_where = total - LAT + lax.broadcasted_iota(jnp.int32, (1, LAT), 1)
    lat_pick = one_hot_t(late[0:1].astype(jnp.int32), lat_where, lat_first, ROWS_KEY + ROWS_OWN)
    q_t = mm(q_high, lat_pick) + mm(q_low, lat_pick)
    q = (q_t * late[1:2] * (HD**-0.5 * LOG2E)).T
    q_high, q_low = halves(q)
    q_ref[...] = jnp.concatenate([q_high, q_high, q_low, q_low], axis=1)

    blocks = span // local
    last = part == parts - 1

    def step(i, masked=False):
        chunk = part * blocks + i
        got = ids_got[chunk]
        pick = one_hot_t(got[0:1].astype(jnp.int32), chunk * local + iota, key_first, 0)
        picked = mm(kv_ref[...], pick)
        both = (picked[0 : 2 * HD] + picked[2 * HD : 4 * HD]) * got[1:2]
        high, low = halves(both)
        keys = jnp.concatenate([high[:HD], low[:HD], high[:HD], low[:HD]], axis=0)
        vals = jnp.concatenate(
            [high[HD:], low[HD:], jnp.ones((2 * HD, local), NARROW)], axis=0
        )
        scores = mm(q_ref[...], keys)
        if masked:
            lane = lax.broadcasted_iota(jnp.int32, (LAT, local), 1) - (local - LAT)
            lat = lax.broadcasted_iota(jnp.int32, (LAT, local), 0)
            scores = jnp.where((lane <= lat) | jnp.logical_not(last), scores, -1e30)
        old = top_ref[:, 0:1]
        new = jnp.maximum(old, jnp.max(scores, axis=1, keepdims=True))
        probs = jnp.exp2(scores - new)
        p_high, p_low = halves(probs)
        dims = (((1,), (1,)), ((), ()))
        acc_ref[...] = acc_ref[...] * jnp.exp2(old - new) + (
            mm(p_high, vals, dims) + mm(p_low, vals, dims)
        )
        top_ref[...] = jnp.broadcast_to(new, top_ref.shape)

    def body(i, carry):
        step(i)
        return carry

    half = blocks // 2
    lax.fori_loop(0, half, body, 0)
    own.wait()
    for copy in wz_copies:
        copy.wait()
    for k, ss in enumerate(flat):
        line = wo_out_ref.at[:, s]
        copies.append(send(line, line, (wp_send, wp_recv), k, z * inner + ss, head))
    lax.fori_loop(half, blocks - 1, body, 0)
    step(blocks - 1, True)

    acc = acc_ref[...]
    state_ref[...] = jnp.concatenate(
        [acc[:, :HD] + acc[:, HD : 2 * HD], acc[:, 2 * HD : 2 * HD + 32], top_ref[:, 0:32]],
        axis=1,
    )
    rows = LAT // n_pos

    def latents_of(peer):
        return pl.ds(pl.multiple_of(peer * rows, rows), rows)

    for k, peer in enumerate(peers):
        copies.append(
            send(state_ref.at[latents_of(peer)], got_ref.at[me], (st_send, st_recv), k, peer, head)
        )
    got_ref[me] = state_ref[latents_of(me), :]
    for copy in copies:
        copy.wait()
    out_ref[...] = got_ref[...]


def mlp_kernel(
    n_pos, heads, outer, heads_dev, in_rows, states_ref, wo_ref, mlp_ref, out_ref,
    sums, lanes, full, other, other_got, red, red_got, mid, mid_got, last,
    s0, r0, s1, r1, s2, r2, s3, r3, s4, r4, s5, r5, s6, r6, s7, r7,
):
    inner = n_pos // outer
    me, head = lax.axis_index("pos"), lax.axis_index("head")
    z, s = me // inner, lax.rem(me, inner)
    cols = full.shape[-1]
    lat = n_pos * full.shape[3]
    siblings = [lax.rem(head + k, heads) for k in range(1, heads)]
    deep = [lax.rem(z + k, outer) for k in range(1, outer)]
    flat = [lax.rem(s + k, inner) for k in range(1, inner)]
    greet(
        [(me, h) for h in siblings]
        + [(zz * inner + s, head) for zz in deep]
        + [(z * inner + ss, head) for ss in flat]
    )

    parts = n_pos // heads_dev
    attended = []
    for slot in range(heads_dev):
        own = [states_ref[slot * parts + p] for p in range(parts)]
        top = own[0][:, 96:97]
        for state in own[1:]:
            top = jnp.maximum(top, state[:, 96:97])
        mixed = sum(state * jnp.exp2(state[:, 96:97] - top) for state in own)
        attended.append(mixed[:, :HD] / mixed[:, HD : HD + 1])
    attended = jnp.concatenate(attended, axis=1)
    sums[head] = mm3(attended, wo_ref[...], (((1,), (1,)), ((), ())))
    copies = [
        send(sums.at[head], sums.at[head], (s0, r0), k, me, h) for k, h in enumerate(siblings)
    ]
    for copy in copies:
        copy.wait()
    projected = sums[0]
    for h in range(1, heads):
        projected = projected + sums[h]
    normed = layer_norm(projected)
    for h in range(heads):
        lanes[h] = normed[:, h * cols : (h + 1) * cols]
    full[head, z, s] = lanes[head]

    mine = full.at[head, z, s]
    copies = [
        send(mine, mine, (s1, r1), k, zz * inner + s, head) for k, zz in enumerate(deep)
    ]
    for copy in copies:
        copy.wait()
    mine = full.at[head, :, s]
    copies = [
        send(mine, mine, (s2, r2), k, z * inner + ss, head) for k, ss in enumerate(flat)
    ]
    across = [
        send(mine, mine, (s3, r3), k * inner, me, h) for k, h in enumerate(siblings)
    ]
    for j, copy in enumerate(copies):
        copy.wait()
        came = full.at[head, :, lax.rem(s - (j + 1) + inner, inner)]
        across += [
            send(came, came, (s3, r3), k * inner + j + 1, me, h)
            for k, h in enumerate(siblings)
        ]

    def weights(h, first):
        mine = mlp_ref[pl.ds(h * (n_pos // heads), n_pos // heads), first : first + in_rows, :]
        return mine.reshape(cols, mine.shape[-1])

    def hidden_from(h):
        return mm3(full[h].reshape(lat, cols), weights(h, 0))

    hidden = hidden_from(head)
    for copy in across:
        copy.wait()
    for h in siblings:
        hidden = hidden + hidden_from(h)
    cube = hidden * hidden * hidden
    hidden = 0.5 * hidden * (1.0 + jnp.tanh(0.7978845608028654 * (hidden + 0.044715 * cube)))

    def down_to(h):
        return mm3(hidden, weights(h, in_rows), (((1,), (1,)), ((), ())))

    copies = []
    for k, h in enumerate(siblings):
        other[k] = down_to(h)
        copies.append(send(other.at[k], other_got.at[k], (s4, r4), k, me, h))
    total = down_to(head)
    for k, copy in enumerate(copies):
        copy.wait()
        total = total + other_got[k]
    red[...] = total.reshape(red.shape)

    copies = [
        send(red.at[:, ss], red_got.at[k], (s5, r5), k, z * inner + ss, head)
        for k, ss in enumerate(flat)
    ]
    total = red[:, s]
    for k, copy in enumerate(copies):
        copy.wait()
        total = total + red_got[k]
    mid[...] = total
    copies = [
        send(mid.at[zz], mid_got.at[k], (s6, r6), k, zz * inner + s, head)
        for k, zz in enumerate(deep)
    ]
    total = mid[z]
    for k, copy in enumerate(copies):
        copy.wait()
        total = total + mid_got[k]
    last[head] = total
    copies = [
        send(last.at[head], last.at[head], (s7, r7), k, me, h) for k, h in enumerate(siblings)
    ]
    for copy in copies:
        copy.wait()
    out_ref[...] = projected + jnp.concatenate([last[h] for h in range(heads)], axis=1)


def layer_norm(values):
    center = values - jnp.mean(values, axis=-1, keepdims=True)
    spread = jnp.mean(center * center, axis=-1, keepdims=True)
    return center * lax.rsqrt(spread + 1e-05)


def per_device(
    token_ids,
    token_table,
    row_table,
    col_table,
    chan_table,
    w_query,
    w_key,
    w_value,
    w_out,
    w_in,
    w_down,
):
    local = token_ids.shape[0]
    n_pos = lax.axis_size("pos")
    heads_dev = w_key.shape[1] // HD
    parts = n_pos // heads_dev
    depth = token_table.shape[1]
    outer = 4 if n_pos % 4 == 0 else 1
    inner = n_pos // outer
    vmem = pl.BlockSpec(memory_space=pltpu.VMEM)
    hbm = pl.BlockSpec(memory_space=pl.ANY)
    dma = pltpu.SemaphoreType.DMA

    def room(*shape):
        return pltpu.VMEM(shape, jnp.float32)

    ff_rows = w_in.shape[1] // n_pos
    lat_rows = LAT // n_pos
    moves = ff_rows % 128 == 0
    mlp_weights = jnp.concatenate([w_in, w_down.T])
    if not moves:
        mlp_kept = lax.all_to_all(
            mlp_weights.reshape(-1, n_pos, ff_rows).transpose(1, 0, 2),
            "pos", split_axis=0, concat_axis=0, tiled=True,
        )
        mlp_weights = jnp.zeros((8, 128), jnp.float32)
    mlp_shape = (n_pos, mlp_weights.shape[0], ff_rows) if moves else (8, 128)
    state_shape = (n_pos, lat_rows, 2 * HD)
    out_t = w_out.T
    spots = 2 * IMG + EXTRA
    states, whole_out, mlp_moved = pl.pallas_call(
        functools.partial(front_kernel, n_pos, parts, outer, moves),
        out_shape=[
            jax.ShapeDtypeStruct(state_shape, jnp.float32),
            jax.ShapeDtypeStruct((outer, inner) + out_t.shape, jnp.float32),
            jax.ShapeDtypeStruct(mlp_shape, jnp.float32),
        ],
        in_specs=[vmem] * 5 + [hbm] * 5,
        out_specs=[vmem, hbm, hbm],
        scratch_shapes=[
            room(spots, depth),
            pltpu.VMEM((spots, depth), NARROW),
            pltpu.VMEM((spots, depth), NARROW),
            room(3, depth, 2 * HD),
            room(n_pos, 2, local),
            room(LAT, 4 * HD),
            room(LAT, 128),
            pltpu.VMEM((4 * HD, spots), NARROW),
            pltpu.VMEM((LAT, 4 * HD), NARROW),
            room(LAT, 2 * HD),
            room(*state_shape),
            dma((3,)),
            dma((2,)),
        ]
        + [
            dma((count,))
            for count in (n_pos, outer, inner, n_pos, n_pos)
            for _ in range(2)
        ],
        compiler_params=pltpu.CompilerParams(
            vmem_limit_bytes=48 * 2**20, collective_id=1, has_side_effects=True
        ),
        cost_estimate=pl.CostEstimate(
            flops=20 * 10**9, bytes_accessed=8 * 2**20, transcendentals=4 * 2**20
        ),
    )(
        token_ids[None], token_table, row_table, col_table, chan_table,
        w_key, w_value, w_query, out_t, mlp_weights,
    )
    if moves:
        mlp_kept = mlp_moved
    whole_out = whole_out.reshape(depth, -1)

    heads = lax.axis_size("head")
    cols = depth // heads

    counts = [heads, outer, inner, heads * inner, heads, inner, outer, heads]
    return pl.pallas_call(
        functools.partial(mlp_kernel, n_pos, heads, outer, heads_dev, w_in.shape[0]),
        out_shape=jax.ShapeDtypeStruct((lat_rows, depth), jnp.float32),
        in_specs=[vmem] * 3,
        out_specs=vmem,
        scratch_shapes=[
            room(heads, lat_rows, depth),
            room(heads, lat_rows, cols),
            room(heads, outer, inner, lat_rows, cols),
            room(heads - 1, LAT, cols),
            room(heads - 1, LAT, cols),
            room(outer, inner, lat_rows, cols),
            room(inner - 1, outer, lat_rows, cols),
            room(outer, lat_rows, cols),
            room(outer - 1, lat_rows, cols),
            room(heads, lat_rows, cols),
        ]
        + [dma((count,)) for count in counts for _ in range(2)],
        compiler_params=pltpu.CompilerParams(
            vmem_limit_bytes=48 * 2**20, collective_id=2, has_side_effects=True
        ),
    )(states, whole_out, mlp_kept)


def solution(mesh):
    placed = (
        P("pos"),
        P(),
        P(),
        P(),
        P(),
        P(None, "head"),
        P(None, "head"),
        P(None, "head"),
        P("head", "pos"),
        P("pos", "head"),
        P("head", "pos"),
    )
    return jax.shard_map(
        per_device, mesh=mesh, in_specs=placed, out_specs=P("pos", None), check_vma=False
    )
```

time: 167 us -> 127 us (0.76)
  local copies, waits for them, and re-layouts: 32.6 us -> 5.52 us
  Pallas kernels: 105 us -> 120 us
  between operations: 13.9 us -> 0.04 us
  other arithmetic: 12 us -> 1.42 us
  matrix products: 2.6 us -> 0 us
    concatenate x3 -> x0, local copies, waits for them, and re-layouts: 17.3 us -> none  [the longest x1 8.62 us: per_device(): own_tabs = jnp.concatenate(base + [own_rows] + tail)]
    pallas_call x4 -> x2, Pallas kernels: 105 us -> 120 us  [the longest x1 65.8 us: per_device(): pl.pallas_call(functools.partial(front_kernel, n_pos, parts, outer, moves...]
    dynamic_slice x6 -> x0, local copies, waits for them, and re-layouts: 4.14 us -> none  [the longest x2 1.76 us: of_head(): return lax.dynamic_slice_in_dim(w, head * HD, HD, axis=1)]
    sub x5 -> x0, other arithmetic: 3.94 us -> none  [the longest x3 2.93 us: centered(): return table - jnp.mean(table, axis=-1, keepdims=True)]
    reduce_sum x6 -> x0, other arithmetic: 3.13 us -> none  [the longest x4 2.98 us: centered(): return table - jnp.mean(table, axis=-1, keepdims=True)]
    dot_general x1 -> x0, matrix products: 2.6 us -> none  [per_device(): partial_out = jnp.dot(attended, whole_out, precision=high)]
    slice x3 -> x0, local copies, waits for them, and re-layouts: 2.55 us -> none  [the longest x1 1.28 us: per_device(): my_down = mlp_kept[:, in_rows:].reshape(-1, ff_rows)]
    unnamed x36 -> x15, local copies, waits for them, and re-layouts: 5.51 us -> 5.52 us
  transfers between devices with their start and end apart: 1 -> 0, of which waited for: 0 -> 0; matrix products, arithmetic and copies ran while one was open for 24% -> 0% of each run, Pallas kernels for 32% -> 0%
where the time goes in v1:
time: 127 us
  Pallas kernels  120 us (94%)
  local copies, waits for them, and re-layouts  5.52 us (4%)
  other arithmetic  1.42 us (1%)
    pallas_call x1, Pallas kernels, per_device(): pl.pallas_call(functools.partial(front_kernel, n_pos, parts, outer, moves...  65.8 us
    pallas_call x1, Pallas kernels, per_device(): pl.pallas_call(functools.partial(mlp_kernel, n_pos, heads, outer, heads_d...  53.8 us
    unnamed x15, local copies, waits for them, and re-layouts  5.52 us

profile of v1, /device:TPU:0, one launch (start us, length us, event | category | flops | bytes accessed | tf_op | source)
XLA Modules:
  0.0 126.6 jit_solution(12203540323442165109)
XLA Ops:
  0.0 0.0 copy-start.2
  0.0 0.0 copy-start.1
  0.0 0.0 copy-start.6
  0.0 1.4 %pad_maximum_fusion.mlp_ref = f32[128,2048]{1,0:T(8,128)S(1)} fusion(f32[64,2048]{1,0:T(8,128)} %bitcast.7, f32[64,2048]{1,0:T(8,128)} %param.20), kind=kLoop, calls=%fused_computation | loop fusion | flops 262144 | bytes 2097152 | tf_op jit(solution)/shard_map/concatenate | solution.py:405
  1.4 0.1 copy-done.2
  1.5 0.3 copy-done.1
  1.9 0.0 copy-done.6
  1.9 0.0 copy-start.3
  1.9 1.2 copy-done.3
  3.1 0.0 copy-start.4
  3.1 0.9 copy-done.4
  4.0 0.0 copy-start.5
  4.0 0.7 copy-done.5
  4.7 65.8 %shard_map.109 = (f32[16,32,128]{2,1,0:T(8,128)S(1)}, f32[4,4,64,512]{3,2,1,0:T(8,128)}, f32[16,128,128]{2,1,0:T(8,128)S(1)}) custom-call(s32[1,1024]{1,0:T(1,128)S(1)} %bitcast.6, f32[256,1024]{1,0:T(8,128)S(1)} %copy-done.1, f32[256,1024]{1,0:T(8,128)S(1)} %copy-done.2, f32[256,1024]{1,0:T(8,128)S(1)} %copy-done.3, f32[3,1024]{1,0:T(4,128)S(1)} %copy-done.5, ...), custom_call_target="tpu_custom_call" | custom-call | flops 20000000000 | bytes 8388608 | tf_op jit(solution)/shard_map/pallas_call | solution.py:416
  70.6 0.0 copy-start
  70.6 1.6 %copy-done = f32[4,4,64,512]{3,2,1,0:T(8,128)S(1)} copy-done((f32[4,4,64,512]{3,2,1,0:T(8,128)S(1)}, f32[4,4,64,512]{3,2,1,0:T(8,128)}, u32[]{:S(2)}) %copy-start) | copy-done | bytes 2097176
  72.2 53.8 %shard_map.110 = f32[32,1024]{1,0:T(8,128)S(1)} custom-call(f32[16,32,128]{2,1,0:T(8,128)S(1)} %get-tuple-element.8.states_ref, f32[1024,512]{1,0:T(8,128)S(1)} %bitcast.4, f32[16,128,128]{2,1,0:T(8,128)S(1)} %get-tuple-element.10.mlp_ref), custom_call_target="tpu_custom_call" | custom-call | tf_op jit(solution)/shard_map/pallas_call | solution.py:463
  126.0 0.7 copy.13
Async XLA Ops:
  0.0 1.5 %copy-start.2 = (f32[256,1024]{1,0:T(8,128)S(1)}, f32[256,1024]{1,0:T(8,128)}, u32[]{:S(2)}) copy-start(f32[256,1024]{1,0:T(8,128)} %row_ref.1) | copy-start | bytes 3145732
  0.0 1.9 %copy-start.1 = (f32[256,1024]{1,0:T(8,128)S(1)}, f32[256,1024]{1,0:T(8,128)}, u32[]{:S(2)}) copy-start(f32[256,1024]{1,0:T(8,128)} %tok_ref.1) | copy-start | bytes 3145732
  0.0 1.9 %copy-start.6 = (s32[1024]{0:T(1024)S(1)}, s32[1024]{0:T(1024)}, u32[]{:S(2)}) copy-start(s32[1024]{0:T(1024)} %param.11) | copy-start | bytes 12292
  1.9 1.2 copy-start.3
  3.1 0.9 copy-start.4
  4.0 0.7 copy-start.5
  70.6 1.6 %copy-start = (f32[4,4,64,512]{3,2,1,0:T(8,128)S(1)}, f32[4,4,64,512]{3,2,1,0:T(8,128)}, u32[]{:S(2)}) copy-start(f32[4,4,64,512]{3,2,1,0:T(8,128)} %get-tuple-element.9) | copy-start | bytes 6291460

commit v2 on v1

--- a/solution.py
+++ b/solution.py
@@ -73,13 +73,14 @@
     return jnp.concatenate([tok, col, pair], axis=0)
 
 
-def front_kernel(
-    n_pos, parts, outer, moves,
+def layer_kernel(
+    n_pos, heads, parts, outer, in_rows, moves,
     ids_ref, tok_ref, row_ref, col_ref, chan_ref, wk_ref, wv_ref, wq_ref, wo_ref, mlp_ref,
     out_ref, wo_out_ref, mlp_out_ref,
-    tabs_ref, high_ref, low_ref, w_ref, ids_got, acc_ref, top_ref, kv_ref, q_ref, state_ref,
+    sums, lanes, full, other, other_got, red, red_got, mid, mid_got, fin, tabs_ref, high_ref, low_ref, w_ref, ids_got, acc_ref, top_ref, kv_ref, q_ref, state_ref,
     got_ref, w_sem, own_sem, id_send, id_recv, wz_send, wz_recv, wp_send, wp_recv,
-    mlp_send, mlp_recv, st_send, st_recv,
+    mlp_send, mlp_recv, st_send, st_recv, s0, r0, s1, r1, s2, r2, s3, r3, s4, r4, s5, r5,
+    s6, r6, s7, r7,
 ):
     inner = n_pos // outer
     me, head = lax.axis_index("pos"), lax.axis_index("head")
@@ -87,7 +88,8 @@
     peers = [lax.rem(me + k, n_pos) for k in range(1, n_pos)]
     deep = [lax.rem(z + k, outer) for k in range(1, outer)]
     flat = [lax.rem(s + k, inner) for k in range(1, inner)]
-    greet([(peer, head) for peer in peers])
+    siblings = [lax.rem(head + k, heads) for k in range(1, heads)]
+    greet([(peer, head) for peer in peers] + [(me, h) for h in siblings])
     local = ids_ref.shape[1]
     total = local * n_pos
     span = total // parts
@@ -113,8 +115,8 @@
     tabs_ref[2 * IMG + CHAN_AT : 2 * IMG + CHAN_AT + 3, :] = chan_ref[...]
     extra = jnp.concatenate([key_rows, own_rows, lat_rows, tabs_ref[2 * IMG + CHAN_AT :, :]])
     for k, table in enumerate((tok_ref[...], col_ref[...], extra)):
-        mid = table - jnp.mean(table, axis=1, keepdims=True)
-        high, low = halves(mid)
+        middle = table - jnp.mean(table, axis=1, keepdims=True)
+        high, low = halves(middle)
         high_ref[k * IMG : k * IMG + table.shape[0], :] = high
         low_ref[k * IMG : k * IMG + table.shape[0], :] = low
 
@@ -140,21 +142,6 @@
         send(wo_ref, wo_out_ref.at[z, s], (wz_send, wz_recv), k, zz * inner + s, head)
         for k, zz in enumerate(deep)
     ]
-    copies = []
-    if moves:
-        wide = mlp_ref.shape[1] // n_pos
-
-        def slab(peer):
-            return mlp_ref.at[:, pl.ds(pl.multiple_of(peer * wide, wide), wide)]
-
-        for k, peer in enumerate(peers):
-            copies.append(
-                send(slab(peer), mlp_out_ref.at[me], (mlp_send, mlp_recv), k, peer, head)
-            )
-        kept = pltpu.make_async_copy(slab(me), mlp_out_ref.at[me], own_sem.at[1])
-        kept.start()
-        copies.append(kept)
-
     for load in loads:
         load.wait()
     even = lax.rem(slot, 2) == 0
@@ -217,14 +204,30 @@
         step(i)
         return carry
 
-    half = blocks // 2
+    half = blocks // 4
     lax.fori_loop(0, half, body, 0)
     own.wait()
     for copy in wz_copies:
         copy.wait()
-    for k, ss in enumerate(flat):
-        line = wo_out_ref.at[:, s]
-        copies.append(send(line, line, (wp_send, wp_recv), k, z * inner + ss, head))
+    line = wo_out_ref.at[:, s]
+    wo_copies = [
+        send(line, line, (wp_send, wp_recv), k, z * inner + ss, head)
+        for k, ss in enumerate(flat)
+    ]
+    mlp_copies = []
+    if moves:
+        wide = mlp_ref.shape[1] // n_pos
+
+        def slab(peer):
+            return mlp_ref.at[:, pl.ds(pl.multiple_of(peer * wide, wide), wide)]
+
+        for k, peer in enumerate(peers):
+            mlp_copies.append(
+                send(slab(peer), mlp_out_ref.at[me], (mlp_send, mlp_recv), k, peer, head)
+            )
+        kept = pltpu.make_async_copy(slab(me), mlp_out_ref.at[me], own_sem.at[1])
+        kept.start()
+        mlp_copies.append(kept)
     lax.fori_loop(half, blocks - 1, body, 0)
     step(blocks - 1, True)
 
@@ -238,46 +241,25 @@
     def latents_of(peer):
         return pl.ds(pl.multiple_of(peer * rows, rows), rows)
 
-    for k, peer in enumerate(peers):
-        copies.append(
-            send(state_ref.at[latents_of(peer)], got_ref.at[me], (st_send, st_recv), k, peer, head)
-        )
+    copies = [
+        send(state_ref.at[latents_of(peer)], got_ref.at[me], (st_send, st_recv), k, peer, head)
+        for k, peer in enumerate(peers)
+    ]
     got_ref[me] = state_ref[latents_of(me), :]
-    for copy in copies:
-        copy.wait()
-    out_ref[...] = got_ref[...]
-
-
-def mlp_kernel(
-    n_pos, heads, outer, heads_dev, in_rows, states_ref, wo_ref, mlp_ref, out_ref,
-    sums, lanes, full, other, other_got, red, red_got, mid, mid_got, last,
-    s0, r0, s1, r1, s2, r2, s3, r3, s4, r4, s5, r5, s6, r6, s7, r7,
-):
-    inner = n_pos // outer
-    me, head = lax.axis_index("pos"), lax.axis_index("head")
-    z, s = me // inner, lax.rem(me, inner)
-    cols = full.shape[-1]
-    lat = n_pos * full.shape[3]
-    siblings = [lax.rem(head + k, heads) for k in range(1, heads)]
-    deep = [lax.rem(z + k, outer) for k in range(1, outer)]
-    flat = [lax.rem(s + k, inner) for k in range(1, inner)]
-    greet(
-        [(me, h) for h in siblings]
-        + [(zz * inner + s, head) for zz in deep]
-        + [(z * inner + ss, head) for ss in flat]
-    )
-
-    parts = n_pos // heads_dev
+    for copy in copies + wo_copies:
+        copy.wait()
+
     attended = []
-    for slot in range(heads_dev):
-        own = [states_ref[slot * parts + p] for p in range(parts)]
+    for first in range(0, n_pos, parts):
+        own = [got_ref[first + p] for p in range(parts)]
         top = own[0][:, 96:97]
         for state in own[1:]:
             top = jnp.maximum(top, state[:, 96:97])
         mixed = sum(state * jnp.exp2(state[:, 96:97] - top) for state in own)
         attended.append(mixed[:, :HD] / mixed[:, HD : HD + 1])
     attended = jnp.concatenate(attended, axis=1)
-    sums[head] = mm3(attended, wo_ref[...], (((1,), (1,)), ((), ())))
+    whole_out = wo_out_ref[...].reshape(depth, attended.shape[1])
+    sums[head] = mm3(attended, whole_out, (((1,), (1,)), ((), ())))
     copies = [
         send(sums.at[head], sums.at[head], (s0, r0), k, me, h) for k, h in enumerate(siblings)
     ]
@@ -287,83 +269,117 @@
     for h in range(1, heads):
         projected = projected + sums[h]
     normed = layer_norm(projected)
+    cols = full.shape[-1]
     for h in range(heads):
         lanes[h] = normed[:, h * cols : (h + 1) * cols]
     full[head, z, s] = lanes[head]
 
+    chunks = [lax.rem(z - k + outer, outer) for k in range(outer)]
     mine = full.at[head, z, s]
+    arrive = [
+        send(mine, mine, (s1, r1), k, zz * inner + s, head) for k, zz in enumerate(deep)
+    ]
+    in_plane, in_chip, halfway, spread = [], [], [], []
+
+    def pass_on(k):
+        if k > 0:
+            arrive[k - 1].wait()
+        came = full.at[head, chunks[k], s]
+        in_plane.append(
+            [
+                send(came, came, (s2, r2), k * inner + j, z * inner + ss, head)
+                for j, ss in enumerate(flat)
+            ]
+        )
+
+    def to_chip(k):
+        for copy in in_plane[k]:
+            copy.wait()
+        came = full.at[head, chunks[k]]
+        in_chip.append(
+            [
+                send(came, came, (s3, r3), k * heads + j, me, h)
+                for j, h in enumerate(siblings)
+            ]
+        )
+
+    kept_ref = mlp_out_ref if moves else mlp_ref
+
+    def weights(h, first):
+        count = n_pos // heads
+        held = kept_ref[pl.ds(h * count, count), first : first + in_rows, :]
+        return held.reshape(cols, held.shape[-1])
+
+    tall = LAT // outer
+
+    def compute(k):
+        for copy in in_chip[k]:
+            copy.wait()
+        hidden = None
+        for h in [head] + siblings:
+            term = mm3(full[h, chunks[k]].reshape(tall, cols), weights(h, 0))
+            hidden = term if hidden is None else hidden + term
+        cube = hidden * hidden * hidden
+        hidden = 0.5 * hidden * (
+            1.0 + jnp.tanh(0.7978845608028654 * (hidden + 0.044715 * cube))
+        )
+        dims = (((1,), (1,)), ((), ()))
+        sent = []
+        for j, h in enumerate(siblings):
+            other[k, j] = mm3(hidden, weights(h, in_rows), dims)
+            sent.append(
+                send(other.at[k, j], other_got.at[k, j], (s4, r4), k * heads + j, me, h)
+            )
+        halfway.append(sent)
+        red[k] = mm3(hidden, weights(head, in_rows), dims).reshape(red.shape[1:])
+
+    def to_plane(k):
+        whole = red[k].reshape(tall, cols)
+        for j, copy in enumerate(halfway[k]):
+            copy.wait()
+            whole = whole + other_got[k, j]
+        red[k] = whole.reshape(red.shape[1:])
+        spread.append(
+            [
+                send(red.at[k, ss], red_got.at[k, j], (s5, r5), k * inner + j,
+                     z * inner + ss, head)
+                for j, ss in enumerate(flat)
+            ]
+        )
+
+    final = []
+
+    def to_owner(k):
+        whole = red[k, s]
+        for j, copy in enumerate(spread[k]):
+            copy.wait()
+            whole = whole + red_got[k, j]
+        mid[k] = whole
+        if k > 0:
+            final.append(
+                send(mid.at[k], mid_got.at[k], (s6, r6), k, chunks[k] * inner + s, head)
+            )
+
+    for k in range(outer):
+        pass_on(k)
+    to_chip(0)
+    for copy in mlp_copies:
+        copy.wait()
+    for t in range(1, outer + 3):
+        for stage, late_by in ((to_chip, 0), (compute, 1), (to_plane, 2), (to_owner, 3)):
+            if 0 <= t - late_by < outer:
+                stage(t - late_by)
+    whole = mid[0]
+    for k, copy in enumerate(final):
+        copy.wait()
+        whole = whole + mid_got[k + 1]
+    fin[head] = whole
     copies = [
-        send(mine, mine, (s1, r1), k, zz * inner + s, head) for k, zz in enumerate(deep)
+        send(fin.at[head], fin.at[head], (s7, r7), k, me, h) for k, h in enumerate(siblings)
     ]
     for copy in copies:
         copy.wait()
-    mine = full.at[head, :, s]
-    copies = [
-        send(mine, mine, (s2, r2), k, z * inner + ss, head) for k, ss in enumerate(flat)
-    ]
-    across = [
-        send(mine, mine, (s3, r3), k * inner, me, h) for k, h in enumerate(siblings)
-    ]
-    for j, copy in enumerate(copies):
-        copy.wait()
-        came = full.at[head, :, lax.rem(s - (j + 1) + inner, inner)]
-        across += [
-            send(came, came, (s3, r3), k * inner + j + 1, me, h)
-            for k, h in enumerate(siblings)
-        ]
-
-    def weights(h, first):
-        mine = mlp_ref[pl.ds(h * (n_pos // heads), n_pos // heads), first : first + in_rows, :]
-        return mine.reshape(cols, mine.shape[-1])
-
-    def hidden_from(h):
-        return mm3(full[h].reshape(lat, cols), weights(h, 0))
-
-    hidden = hidden_from(head)
-    for copy in across:
-        copy.wait()
-    for h in siblings:
-        hidden = hidden + hidden_from(h)
-    cube = hidden * hidden * hidden
-    hidden = 0.5 * hidden * (1.0 + jnp.tanh(0.7978845608028654 * (hidden + 0.044715 * cube)))
-
-    def down_to(h):
-        return mm3(hidden, weights(h, in_rows), (((1,), (1,)), ((), ())))
-
-    copies = []
-    for k, h in enumerate(siblings):
-        other[k] = down_to(h)
-        copies.append(send(other.at[k], other_got.at[k], (s4, r4), k, me, h))
-    total = down_to(head)
-    for k, copy in enumerate(copies):
-        copy.wait()
-        total = total + other_got[k]
-    red[...] = total.reshape(red.shape)
-
-    copies = [
-        send(red.at[:, ss], red_got.at[k], (s5, r5), k, z * inner + ss, head)
-        for k, ss in enumerate(flat)
-    ]
-    total = red[:, s]
-    for k, copy in enumerate(copies):
-        copy.wait()
-        total = total + red_got[k]
-    mid[...] = total
-    copies = [
-        send(mid.at[zz], mid_got.at[k], (s6, r6), k, zz * inner + s, head)
-        for k, zz in enumerate(deep)
-    ]
-    total = mid[z]
-    for k, copy in enumerate(copies):
-        copy.wait()
-        total = total + mid_got[k]
-    last[head] = total
-    copies = [
-        send(last.at[head], last.at[head], (s7, r7), k, me, h) for k, h in enumerate(siblings)
-    ]
-    for copy in copies:
-        copy.wait()
-    out_ref[...] = projected + jnp.concatenate([last[h] for h in range(heads)], axis=1)
+    out_ref[...] = projected + jnp.concatenate([fin[h] for h in range(heads)], axis=1)
 
 
 def layer_norm(values):
@@ -408,21 +424,34 @@
             mlp_weights.reshape(-1, n_pos, ff_rows).transpose(1, 0, 2),
             "pos", split_axis=0, concat_axis=0, tiled=True,
         )
-        mlp_weights = jnp.zeros((8, 128), jnp.float32)
-    mlp_shape = (n_pos, mlp_weights.shape[0], ff_rows) if moves else (8, 128)
-    state_shape = (n_pos, lat_rows, 2 * HD)
+        mlp_weights = mlp_kept
+    mlp_shape = (n_pos, w_in.shape[0] * 2, ff_rows) if moves else (1, 8, 128)
     out_t = w_out.T
     spots = 2 * IMG + EXTRA
-    states, whole_out, mlp_moved = pl.pallas_call(
-        functools.partial(front_kernel, n_pos, parts, outer, moves),
-        out_shape=[
-            jax.ShapeDtypeStruct(state_shape, jnp.float32),
-            jax.ShapeDtypeStruct((outer, inner) + out_t.shape, jnp.float32),
-            jax.ShapeDtypeStruct(mlp_shape, jnp.float32),
-        ],
-        in_specs=[vmem] * 5 + [hbm] * 5,
-        out_specs=[vmem, hbm, hbm],
+    heads = lax.axis_size("head")
+    cols = depth // heads
+    tall = LAT // outer
+    counts = [n_pos, outer, inner, n_pos, n_pos]
+    counts += [heads, outer, outer * inner, outer * heads, outer * heads, outer * inner]
+    counts += [outer, heads]
+    return pl.pallas_call(
+        functools.partial(layer_kernel, n_pos, heads, parts, outer, w_in.shape[0], moves),
+        out_shape=jax.ShapeDtypeStruct((lat_rows, depth), jnp.float32),
+        in_specs=[vmem] * 5 + [hbm] * 4 + [hbm if moves else vmem],
+        out_specs=vmem,
         scratch_shapes=[
+            room(outer, inner, *out_t.shape),
+            room(*mlp_shape),
+            room(heads, lat_rows, depth),
+            room(heads, lat_rows, cols),
+            room(heads, outer, inner, lat_rows, cols),
+            room(outer, heads - 1, tall, cols),
+            room(outer, heads - 1, tall, cols),
+            room(outer, inner, lat_rows, cols),
+            room(outer, inner - 1, lat_rows, cols),
+            room(outer, lat_rows, cols),
+            room(outer, lat_rows, cols),
+            room(heads, lat_rows, cols),
             room(spots, depth),
             pltpu.VMEM((spots, depth), NARROW),
             pltpu.VMEM((spots, depth), NARROW),
@@ -433,55 +462,18 @@
             pltpu.VMEM((4 * HD, spots), NARROW),
             pltpu.VMEM((LAT, 4 * HD), NARROW),
             room(LAT, 2 * HD),
-            room(*state_shape),
+            room(n_pos, lat_rows, 2 * HD),
             dma((3,)),
             dma((2,)),
         ]
-        + [
-            dma((count,))
-            for count in (n_pos, outer, inner, n_pos, n_pos)
-            for _ in range(2)
-        ],
+        + [dma((count,)) for count in counts for _ in range(2)],
         compiler_params=pltpu.CompilerParams(
             vmem_limit_bytes=48 * 2**20, collective_id=1, has_side_effects=True
-        ),
-        cost_estimate=pl.CostEstimate(
-            flops=20 * 10**9, bytes_accessed=8 * 2**20, transcendentals=4 * 2**20
         ),
     )(
         token_ids[None], token_table, row_table, col_table, chan_table,
         w_key, w_value, w_query, out_t, mlp_weights,
     )
-    if moves:
-        mlp_kept = mlp_moved
-    whole_out = whole_out.reshape(depth, -1)
-
-    heads = lax.axis_size("head")
-    cols = depth // heads
-
-    counts = [heads, outer, inner, heads * inner, heads, inner, outer, heads]
-    return pl.pallas_call(
-        functools.partial(mlp_kernel, n_pos, heads, outer, heads_dev, w_in.shape[0]),
-        out_shape=jax.ShapeDtypeStruct((lat_rows, depth), jnp.float32),
-        in_specs=[vmem] * 3,
-        out_specs=vmem,
-        scratch_shapes=[
-            room(heads, lat_rows, depth),
-            room(heads, lat_rows, cols),
-            room(heads, outer, inner, lat_rows, cols),
-            room(heads - 1, LAT, cols),
-            room(heads - 1, LAT, cols),
-            room(outer, inner, lat_rows, cols),
-            room(inner - 1, outer, lat_rows, cols),
-            room(outer, lat_rows, cols),
-            room(outer - 1, lat_rows, cols),
-            room(heads, lat_rows, cols),
-        ]
-        + [dma((count,)) for count in counts for _ in range(2)],
-        compiler_params=pltpu.CompilerParams(
-            vmem_limit_bytes=48 * 2**20, collective_id=2, has_side_effects=True
-        ),
-    )(states, whole_out, mlp_kept)
 
 
 def solution(mesh):

time: 127 us -> 108 us (0.85)
  Pallas kernels: 120 us -> 102 us
  local copies, waits for them, and re-layouts: 5.52 us -> 3.93 us
    pallas_call x2 -> x1, Pallas kernels: 120 us -> 102 us  [per_device(): pl.pallas_call(functools.partial(layer_kernel, n_pos, heads, parts, outer...]
    unnamed x15 -> x13, local copies, waits for them, and re-layouts: 5.52 us -> 3.93 us
where the time goes in v2:
time: 108 us
  Pallas kernels  102 us (94%)
  local copies, waits for them, and re-layouts  3.93 us (4%)
  other arithmetic  1.42 us (1%)
    pallas_call x1, Pallas kernels, per_device(): pl.pallas_call(functools.partial(layer_kernel, n_pos, heads, parts, outer...  102 us
    unnamed x13, local copies, waits for them, and re-layouts  3.93 us

profile of v2, /device:TPU:0, one launch (start us, length us, event | category | flops | bytes accessed | tf_op | source)
XLA Modules:
  0.0 107.6 jit_solution(6341235889514776926)
XLA Ops:
  0.0 0.0 copy-start.1
  0.0 0.0 copy-start
  0.0 0.0 copy-start.5
  0.0 1.4 %pad_maximum_fusion.mlp_ref = f32[128,2048]{1,0:T(8,128)S(1)} fusion(f32[64,2048]{1,0:T(8,128)} %bitcast.5, f32[64,2048]{1,0:T(8,128)} %param.20), kind=kLoop, calls=%fused_computation | loop fusion | flops 262144 | bytes 2097152 | tf_op jit(solution)/shard_map/concatenate | solution.py:421
  1.4 0.1 copy-done.1
  1.5 0.3 copy-done
  1.9 0.0 copy-done.5
  1.9 0.0 copy-start.2
  1.9 1.2 %copy-done.2 = f32[256,1024]{1,0:T(8,128)S(1)} copy-done((f32[256,1024]{1,0:T(8,128)S(1)}, f32[256,1024]{1,0:T(8,128)}, u32[]{:S(2)}) %copy-start.2) | copy-done | bytes 1048600
  3.1 0.0 copy-start.3
  3.1 0.9 copy-done.3
  4.0 0.0 copy-start.4
  4.0 0.7 copy-done.4
  4.7 102.2 %shard_map.109 = f32[32,1024]{1,0:T(8,128)S(1)} custom-call(s32[1,1024]{1,0:T(1,128)S(1)} %bitcast.4, f32[256,1024]{1,0:T(8,128)S(1)} %copy-done, f32[256,1024]{1,0:T(8,128)S(1)} %copy-done.1, f32[256,1024]{1,0:T(8,128)S(1)} %copy-done.2, f32[3,1024]{1,0:T(4,128)S(1)} %copy-done.4, f32[1024,512]{1,0:T(8,128)} %wk_ref.1, f32[1024,512]{1,0:T(8,128)} %wv_ref.1, ...), custom_call_target="tpu_custom_call" | custom-call | tf_op jit(solution)/shard_map/pallas_call | solution.py:437
  106.9 0.7 copy.13
Async XLA Ops:
  0.0 1.5 %copy-start.1 = (f32[256,1024]{1,0:T(8,128)S(1)}, f32[256,1024]{1,0:T(8,128)}, u32[]{:S(2)}) copy-start(f32[256,1024]{1,0:T(8,128)} %row_ref.1) | copy-start | bytes 3145732
  0.0 1.9 %copy-start = (f32[256,1024]{1,0:T(8,128)S(1)}, f32[256,1024]{1,0:T(8,128)}, u32[]{:S(2)}) copy-start(f32[256,1024]{1,0:T(8,128)} %tok_ref.1) | copy-start | bytes 3145732
  0.0 1.9 %copy-start.5 = (s32[1024]{0:T(1024)S(1)}, s32[1024]{0:T(1024)}, u32[]{:S(2)}) copy-start(s32[1024]{0:T(1024)} %param.11) | copy-start | bytes 12292
  1.9 1.2 %copy-start.2 = (f32[256,1024]{1,0:T(8,128)S(1)}, f32[256,1024]{1,0:T(8,128)}, u32[]{:S(2)}) copy-start(f32[256,1024]{1,0:T(8,128)} %col_ref.1) | copy-start | bytes 3145732
  3.1 0.9 copy-start.3
  4.0 0.7 copy-start.4
